TPU v7x, 32 devices: a whole 2x2x4 slice. The times are simulated.
32 devices in a mesh: groups: 2 (over y), blk: 4 (over z), dim: 2 (over x), sub: 2 (over core).
Axes of the slice: x: 2, y: 2, z: 4, core: 2. Of those that a mesh axis runs over, the one named last changes fastest.
Arguments:
- queries: bfloat16 [96, 262144], P('blk', ('dim', 'sub')), may hold values from -6 to 6
- train_slab: bfloat16 [1024, 262144], P(('groups', 'blk'), ('dim', 'sub')), parts along dimension 0, may hold values from -6 to 6
- basis_in: bfloat16 [64, 64, 64], P(('dim', 'sub')), may hold values from -0.75 to 0.75
- basis_out: bfloat16 [64, 64, 64], P(('dim', 'sub')), may hold values from -0.75 to 0.75
- eigvals: float32 [64, 64, 64], P(('dim', 'sub')), may hold values from 0.2 to 5
- query_ids: int32 [4, 24], replicated, may hold values from 0 to 23, each once within a row
- example_ids: int32 [8, 128], P(('groups', 'blk')), parts along dimension 0, may hold values from 0 to 127, each once within a row
Outputs:
- scores: float32 [96, 1024], P(('dim', 'sub'), ('groups', 'blk')), parts along dimension 1
There are 2 independent parts, one for each index of `groups`. A program takes and returns all parts, laid end to end along the dimension named above; an argument that names none is the same for every part. Nothing has to cross between parts.
Inputs may be any that keep to these rules, and one draw needn't show every extreme that they name: `query_ids`: each row is a permutation of 0 to 23. `example_ids`: each row is a permutation of 0 to 127.
All inputs are finite; a program needn't handle non-finite values.
Results may differ from a plain program's by a relative error of at most 0.0029.
Values may be sent and summed in bfloat16 or wider, within the bound.
A program may use at most 128 MiB of HBM per device.

v0:
```python
import jax
import jax.numpy as jnp
from jax import lax
from jax.sharding import PartitionSpec as P

PROJ = 262144


HIGH = lax.Precision.HIGHEST
DAMPING = 0.01


def precondition(blocks, basis_in, basis_out, eigvals):
    left = basis_in.astype(jnp.float32)
    right = basis_out.astype(jnp.float32)
    inner = jnp.einsum("qbac,bad->qbdc", blocks, left, precision=HIGH)
    inner = jnp.einsum("qbdc,bce->qbde", inner, right, precision=HIGH)
    inner = inner / (eigvals + DAMPING)[None]
    outer = jnp.einsum("qbde,bad->qbae", inner, left, precision=HIGH)
    return jnp.einsum("qbae,bce->qbac", outer, right, precision=HIGH)


def slab_scores(rows, slab_rows):
    return lax.dot_general(
        rows, slab_rows, (((1,), (1,)), ((), ())), preferred_element_type=jnp.float32
    )


def prepared(span_rows, span_ids, basis_in, basis_out, eigvals):
    count = span_rows.shape[0]
    width = span_rows.shape[1]
    blocks = span_rows.astype(jnp.float32).reshape(
        count, basis_in.shape[0], basis_in.shape[1], basis_out.shape[1]
    )
    precond = precondition(blocks, basis_in, basis_out, eigvals).reshape(count, width)
    query_hot = (span_ids[:, None] == jnp.arange(count, dtype=jnp.int32)[None, :]).astype(
        jnp.float32
    )
    return jnp.einsum("im,ik->mk", query_hot, precond, precision=HIGH).astype(jnp.bfloat16)


def local(queries, train_slab, basis_in, basis_out, eigvals, query_ids, example_ids):
    examples = train_slab.shape[0]
    own_ids = lax.dynamic_index_in_dim(query_ids, lax.axis_index("blk"), 0, keepdims=False)
    ordered = prepared(queries, own_ids, basis_in, basis_out, eigvals)
    partial_value = slab_scores(lax.all_gather(ordered, "blk", axis=0, tiled=True), train_slab)
    summed = lax.psum_scatter(partial_value, ("dim", "sub"), scatter_dimension=0, tiled=True)
    scaled = summed * (1.0 / PROJ**0.5)
    example_hot = (
        example_ids[0][:, None] == jnp.arange(examples, dtype=jnp.int32)[None, :]
    ).astype(jnp.float32)
    return jnp.dot(scaled, example_hot, precision=HIGH, preferred_element_type=jnp.float32)


def solution(mesh):
    return jax.shard_map(
        local,
        mesh=mesh,
        in_specs=(
            P("blk", ("dim", "sub")),
            P(("groups", "blk"), ("dim", "sub")),
            P(("dim", "sub"), None, None),
            P(("dim", "sub"), None, None),
            P(("dim", "sub"), None, None),
            P(),
            P(("groups", "blk"), None),
        ),
        out_specs=P(("dim", "sub"), ("groups", "blk")),
        check_vma=False,
    )
```

profile of v0, /device:TPU:0, one launch (start us, length us, event | category | flops | bytes accessed | tf_op | source)
XLA Modules:
  0.0 343.4 jit_solution(15620766995081679052)
XLA Ops:
  6.5 0.0 copy-start
  6.5 0.0 all-gather.2.cloned.1.call-start
  6.5 0.0 copy-start.2
  6.5 8.4 %reshape.10 = bf16[24,16,64,64]{3,2,1,0:T(8,128)(2,1)} reshape(bf16[24,65536]{1,0:T(8,128)(2,1)} %param.7) | data formatting | bytes 6291456 | tf_op jit(solution)/shard_map/reshape | solution.py:32
  15.0 1.1 broadcast_add_fusion
  16.1 0.0 copy-done
  16.1 4.6 %fusion.7 = f32[16,64,24,64]{3,1,2,0:T(8,128)S(1)} fusion(bf16[24,16,64,64]{3,2,1,0:T(8,128)(2,1)} %reshape.10, bf16[16,64,64]{2,1,0:T(8,128)(2,1)S(1)} %copy-done), kind=kOutput, calls=%fused_computation.8 | convolution fusion | flops 201326592 | bytes 9568256 | tf_op jit(solution)/shard_map/qbac,bad->qbdc/dot_general | solution.py:16
  20.7 0.0 copy-done.2
  20.7 8.3 %fusion.4 = f32[16,24,64,64]{3,2,1,0:T(8,128)} fusion(f32[16,64,24,64]{3,1,2,0:T(8,128)S(1)} %fusion.7, bf16[16,64,64]{2,1,0:T(8,128)(2,1)S(1)} %copy-done.2), kind=kOutput, calls=%fused_computation.5 | convolution fusion | flops 1207959552 | bytes 12713984 | tf_op jit(solution)/shard_map/qbdc,bce->qbde/dot_general | solution.py:17
  29.1 12.8 %fusion.2 = f32[16,24,64,64]{3,2,1,0:T(8,128)S(1)} fusion(f32[16,24,64,64]{3,2,1,0:T(8,128)} %fusion.4, f32[16,64,64]{2,1,0:T(8,128)S(1)} %broadcast_add_fusion, bf16[16,64,64]{2,1,0:T(8,128)(2,1)S(1)} %copy-done), kind=kOutput, calls=%fused_computation.3 | convolution fusion | flops 1209532416 | bytes 12976128 | tf_op jit(solution)/shard_map/qbde,bad->qbae/dot_general | solution.py:19
  41.8 12.8 %fusion.10 = f32[24,16,64,64]{3,2,0,1:T(8,128)} fusion(f32[16,24,64,64]{3,2,1,0:T(8,128)S(1)} %fusion.2, bf16[16,64,64]{2,1,0:T(8,128)(2,1)S(1)} %copy-done.2), kind=kOutput, calls=%fused_computation.11 | convolution fusion | flops 1207959552 | bytes 12713984 | tf_op jit(solution)/shard_map/qbae,bce->qbac/dot_general | solution.py:20
  54.7 11.8 %copy.13 = f32[24,16,64,64]{3,2,1,0:T(8,128)} copy(f32[24,16,64,64]{3,2,0,1:T(8,128)} %fusion.10) | data formatting | bytes 12582912 | tf_op jit(solution)/shard_map/qbae,bce->qbac/transpose | solution.py:20
  66.5 9.7 %reshape.11 = f32[24,65536]{1,0:T(8,128)} reshape(f32[24,16,64,64]{3,2,1,0:T(8,128)} %copy.13) | data formatting | bytes 12582912 | tf_op jit(solution)/shard_map/reshape | solution.py:35
  76.2 0.7 dynamic-slice_bitcast_fusion
  76.9 6.5 %convolution_convert_fusion = bf16[24,65536]{1,0:T(8,128)(2,1)} fusion(f32[24,65536]{1,0:T(8,128)} %reshape.11, s32[24]{0:T(128)S(1)} %dynamic-slice_bitcast_fusion), kind=kOutput, calls=%fused_computation | convolution fusion | flops 454558272 | bytes 9437280 | tf_op jit(solution)/shard_map/im,ik->mk/dot_general | solution.py:39
  83.4 0.0 all-gather.2.cloned.1.call-update
  83.4 0.0 copy-start.3
  83.4 0.0 copy-start.1
  83.4 0.0 reduce-scatter.4.cloned.1.call-start
  83.5 221.0 %all-gather.2.cloned.1.call-done = bf16[96,65536]{1,0:T(8,128)(2,1)} async-done(((bf16[24,65536]{1,0:T(8,128)(2,1)}), bf16[96,65536]{1,0:T(8,128)(2,1)}) %all-gather.2.cloned.1.call-update) | async-done | bytes 12582928 | tf_op jit(solution)/shard_map/all_gather | solution.py:46
  304.4 12.8 %fusion.23 = f32[96,128]{1,0:T(8,128)} fusion(bf16[96,65536]{1,0:T(8,128)(2,1)} %all-gather.2.cloned.1.call-done, bf16[128,65536]{1,0:T(8,128)(2,1)} %param.8), kind=kOutput, calls=%fused_computation.26 | convolution fusion | flops 1610612736 | bytes 29409280 | tf_op jit(solution)/shard_map/dot_general | solution.py:24
  317.2 0.0 reduce-scatter.4.cloned.1.call-update
  317.2 17.8 %reduce-scatter.4.cloned.1.call-done = f32[24,128]{1,0:T(8,128)} async-done(((f32[96,128]{1,0:T(8,128)}), f32[24,128]{1,0:T(8,128)}) %reduce-scatter.4.cloned.1.call-update) | async-done | bytes 12304
  335.0 0.0 copy-done.3
  335.0 1.5 fusion.17
  336.5 0.0 copy-done.1
Async XLA Ops:
  6.5 9.6 %copy-start = (bf16[16,64,64]{2,1,0:T(8,128)(2,1)S(1)}, bf16[16,64,64]{2,1,0:T(8,128)(2,1)}, u32[]{:S(2)}) copy-start(bf16[16,64,64]{2,1,0:T(8,128)(2,1)} %param.9) | copy-start | bytes 393220
  6.5 297.9 %all-gather.2.cloned.1.call-start = ((), (), s32[]{:S(2)}) async-start(), calls=%async_computation.1 | async-start | bytes 15728640 | tf_op jit(solution)/shard_map/all_gather | solution.py:46
  6.5 14.2 %copy-start.2 = (bf16[16,64,64]{2,1,0:T(8,128)(2,1)S(1)}, bf16[16,64,64]{2,1,0:T(8,128)(2,1)}, u32[]{:S(2)}) copy-start(bf16[16,64,64]{2,1,0:T(8,128)(2,1)} %param.10) | copy-start | bytes 393220
  83.4 251.6 %copy-start.3 = (s32[1,128]{1,0:T(1,128)S(1)}, s32[1,128]{1,0:T(1,128)}, u32[]{:S(2)}) copy-start(s32[1,128]{1,0:T(1,128)} %param.13) | copy-start | bytes 1540
  83.4 253.1 %copy-start.1 = (bf16[16,64,64]{2,1,0:T(8,128)(2,1)S(1)}, bf16[16,64,64]{2,1,0:T(8,128)(2,1)}, u32[]{:S(2)}) copy-start(bf16[16,64,64]{2,1,0:T(8,128)(2,1)} %param.9) | copy-start | bytes 393220
  83.4 251.6 %reduce-scatter.4.cloned.1.call-start = ((), (), s32[]{:S(2)}) async-start(), calls=%async_computation.2 | async-start | bytes 61440
Sparse Core Ops, SparseCore 0:
  83.5 220.8 all-gather.1
  317.4 17.5 reduce-scatter.3
where the time goes:
time: 344 us; the launch traced here: 343 us
  waiting for transfers between devices  239 us (69%)
  matrix products  59.3 us (17%)
  local copies, waits for them, and re-layouts  30.7 us (9%)
  between operations  13.5 us (4%)
    all_gather x1, waiting for transfers between devices, local(): lax.all_gather(ordered, 'blk', axis=0, tiled=True)  221 us
    unnamed x3, waiting for transfers between devices  17.8 us
    dot_general x1, matrix products, precondition(): return jnp.einsum('qbae,bce->qbac', outer, right, precision=HIGH)  12.8 us
    dot_general x1, matrix products, precondition(): outer = jnp.einsum('qbde,bad->qbae', inner, left, precision=HIGH)  12.8 us
    dot_general x1, matrix products, slab_scores(): lax.dot_general(rows, slab_rows, (((1,), (1,)), ((), ())), preferred_elem...  12.8 us
    transpose x1, local copies, waits for them, and re-layouts, precondition(): return jnp.einsum('qbae,bce->qbac', outer, right, precision=HIGH)  11.8 us
    reshape x1, local copies, waits for them, and re-layouts, prepared(): precondition(blocks, basis_in, basis_out, eigvals).reshape(count, width)  9.68 us
    reshape x1, local copies, waits for them, and re-layouts, prepared(): span_rows.astype(jnp.float32)  8.45 us
  transfers between devices with their start and end apart: 2, of which 2 were waited for; matrix products, arithmetic and copies ran while one was open for 0% of the time, Pallas kernels for 0%

commit v1 on v0

v1 whole, which is shorter than its diff:
```python
import functools

import jax
import jax.numpy as jnp
from jax import lax
from jax.experimental import pallas as pl
from jax.experimental.pallas import tpu as pltpu
from jax.sharding import PartitionSpec as P

PROJ = 262144
DAMPING = 0.01
MESH = pl.DeviceIdType.MESH
F32 = jnp.float32
BF16 = jnp.bfloat16
SIDE = 64
WIDE = SIDE * SIDE
HALF = WIDE // 2
TILES = WIDE // 128


def parts_of(value):
    high = value.astype(BF16)
    return high, (value - high.astype(F32)).astype(BF16)


def kernel(
    sizes,
    q_hbm, slab_hbm, a_ref, g_ref, eig_ref, qid_ref, eid_ref,
    out_ref,
    q_v, slab, gath, acc, spread, left32, wide, part, landed,
    q_sem, slab_sem, recv_sem, send_sem, red_send, red_recv,
):
    n_grp, n_blk, n_dim, n_sub = sizes
    count = q_hbm.shape[0]
    blocks = a_ref.shape[0]
    per = blocks // n_grp
    n_red = n_dim * n_sub
    y = lax.axis_index("groups")
    z = lax.axis_index("blk")
    dx = lax.axis_index("dim")
    core = lax.axis_index("sub")
    rank = dx * n_sub + core
    has_up = z < n_blk - 1
    has_down = z > 0

    def block_at(plane, t):
        return t * n_grp + plane

    def query_copy(b):
        return pltpu.make_async_copy(
            q_hbm.at[:, pl.ds(pl.multiple_of(b * WIDE, WIDE), WIDE)], q_v.at[b], q_sem.at[b]
        )

    def slab_copy(b):
        cols = pl.ds(pl.multiple_of(b * WIDE, WIDE), WIDE)
        return pltpu.make_async_copy(slab_hbm.at[:, cols], slab.at[:, cols], slab_sem.at[b])

    def order(i):
        turn = i // per
        return block_at(lax.rem(y + turn, n_grp), i - turn * per)

    def start_query(i, carry):
        query_copy(order(i)).start()
        return carry

    def start_slab(i, carry):
        slab_copy(order(i)).start()
        return carry

    lax.fori_loop(0, blocks, start_query, 0)
    lax.fori_loop(0, blocks, start_slab, 0)

    barrier = pltpu.get_barrier_semaphore()

    @pl.when(has_up)
    def _():
        pl.semaphore_signal(barrier, inc=1, device_id={"blk": z + 1}, device_id_type=MESH)

    @pl.when(has_down)
    def _():
        pl.semaphore_signal(barrier, inc=1, device_id={"blk": z - 1}, device_id_type=MESH)

    for step in range(1, n_grp):
        pl.semaphore_signal(
            barrier, inc=1, device_id={"groups": lax.rem(y + step, n_grp)}, device_id_type=MESH
        )

    def peer(step):
        to = lax.rem(rank + step, n_red)
        return to, {"dim": to // n_sub, "sub": lax.rem(to, n_sub)}

    for step in range(1, n_red):
        pl.semaphore_signal(barrier, inc=1, device_id=peer(step)[1], device_id_type=MESH)

    acc[...] = jnp.zeros_like(acc)
    wide[...] = jnp.zeros_like(wide)

    def precondition(b):
        query_copy(b).wait()
        x = q_v[b].astype(F32)
        for i in range(TILES):
            spread[i * count:(i + 1) * count, :] = x[:, i * 128:(i + 1) * 128]
        rows = [spread[pl.ds(q, TILES, stride=count), :] for q in range(count)]
        pairs = count // 2
        lhs = jnp.concatenate(
            [jnp.concatenate([rows[2 * p], rows[2 * p + 1]], axis=1) for p in range(pairs)], axis=0
        ).astype(BF16)
        g = g_ref[b].astype(F32)
        zero = jnp.zeros_like(g)
        low = jnp.concatenate([g, zero], axis=1).astype(BF16)
        high = jnp.concatenate([zero, g], axis=1).astype(BF16)
        wide[0:SIDE, 0:128] = low
        wide[SIDE:2 * SIDE, 128:256] = low
        wide[2 * SIDE:3 * SIDE, 0:128] = high
        wide[3 * SIDE:4 * SIDE, 128:256] = high
        w = wide[...]
        y1 = jnp.dot(lhs, w, preferred_element_type=F32)
        inner = jnp.concatenate(
            [
                jnp.concatenate(
                    [y1[p * TILES:(p + 1) * TILES, 0:128], y1[p * TILES:(p + 1) * TILES, 128:256]],
                    axis=0,
                )
                for p in range(pairs)
            ],
            axis=1,
        )
        left32[...] = a_ref[b].astype(F32)
        left = jnp.concatenate(
            [left32[pl.ds(0, TILES, stride=2), :], left32[pl.ds(1, TILES, stride=2), :]], axis=0
        )
        a_out = left.astype(BF16)
        a_in = left.T.astype(BF16)
        hi, lo = parts_of(inner)
        mid = jnp.dot(a_in, hi, preferred_element_type=F32) + jnp.dot(
            a_in, lo, preferred_element_type=F32
        )
        inv = 1.0 / (eig_ref[b] + DAMPING)
        inv = jnp.concatenate([inv, inv], axis=1)
        mid = jnp.concatenate(
            [mid[:, p * 128:(p + 1) * 128] * inv for p in range(pairs)], axis=1
        )
        hi, lo = parts_of(mid)
        outer = jnp.dot(a_out, hi, preferred_element_type=F32) + jnp.dot(
            a_out, lo, preferred_element_type=F32
        )
        lhs = jnp.concatenate(
            [
                jnp.concatenate(
                    [outer[0:TILES, p * 128:(p + 1) * 128], outer[TILES:, p * 128:(p + 1) * 128]],
                    axis=1,
                )
                for p in range(pairs)
            ],
            axis=0,
        )
        hi, lo = parts_of(lhs)
        nt = (((1,), (1,)), ((), ()))
        res = lax.dot_general(hi, w, nt, preferred_element_type=F32) + lax.dot_general(
            lo, w, nt, preferred_element_type=F32
        )
        for p in range(pairs):
            for k in range(2):
                q = 2 * p + k
                spread[q * TILES:(q + 1) * TILES, :] = res[
                    p * TILES:(p + 1) * TILES, k * 128:(k + 1) * 128
                ]
        cols = [spread[pl.ds(i, count, stride=TILES), :] for i in range(TILES)]
        mine = jnp.concatenate(
            [
                jnp.concatenate(cols[:TILES // 2], axis=1),
                jnp.concatenate(cols[TILES // 2:], axis=1),
            ],
            axis=0,
        )
        gath[z, b] = mine.astype(BF16)

    def dot_in(j, b):
        value = gath[j, b]
        for h in range(2):
            right = slab[:, pl.ds(pl.multiple_of(b * WIDE + h * HALF, HALF), HALF)]
            acc[j, h] += lax.dot_general(
                value, right, (((1,), (1,)), ((), ())), preferred_element_type=F32
            )

    def move(j, b, way):
        if way == 0:
            to = {"blk": z - 1}
        elif way == 1:
            to = {"blk": z + 1}
        else:
            to = {"groups": lax.rem(y + way - 1, n_grp)}
        return pltpu.make_async_remote_copy(
            src_ref=gath.at[j, b],
            dst_ref=gath.at[j, b],
            send_sem=send_sem.at[way, j, b],
            recv_sem=recv_sem.at[j, b],
            device_id=to,
            device_id_type=MESH,
        )

    def across(j, b):
        for step in range(1, n_grp):
            move(j, b, 1 + step).start()

    def along(dist, t):
        b = block_at(y, t)

        @pl.when(z + dist < n_blk)
        def _():
            move(z + dist, b, 0).wait_recv()

            @pl.when(has_down)
            def _():
                move(z + dist, b, 0).start()

            across(z + dist, b)

        @pl.when(z - dist >= 0)
        def _():
            move(z - dist, b, 1).wait_recv()

            @pl.when(has_up)
            def _():
                move(z - dist, b, 1).start()

            across(z - dist, b)

        @pl.when(z + dist < n_blk)
        def _():
            dot_in(z + dist, b)

        @pl.when(z - dist >= 0)
        def _():
            dot_in(z - dist, b)

    def beside(dist, t):
        for step in range(1, n_grp):
            b = block_at(lax.rem(y + step, n_grp), t)

            @pl.when(z + dist < n_blk)
            def _():
                move(z + dist, b, 2).wait_recv()
                dot_in(z + dist, b)

            @pl.when(z - dist >= 0)
            def _():
                move(z - dist, b, 2).wait_recv()
                dot_in(z - dist, b)

    def send_own(b):
        @pl.when(has_down)
        def _():
            move(z, b, 0).start()

        @pl.when(has_up)
        def _():
            move(z, b, 1).start()

    def own(i):
        b = order(i)
        precondition(b)

        @pl.when(i < per)
        def _():
            send_own(b)

        return b

    entry = n_grp - 1 + n_red - 1
    pl.semaphore_wait(barrier, entry + has_up.astype(jnp.int32) + has_down.astype(jnp.int32))

    own_per_step = blocks // per

    def first(t, carry):
        def one(k, inner):
            own(t * own_per_step + k)
            return inner

        lax.fori_loop(0, own_per_step, one, 0)

        @pl.when(t == 0)
        def _():
            def wait_slab(i, inner):
                slab_copy(order(i)).wait()
                return inner

            lax.fori_loop(0, blocks, wait_slab, 0)

        def own_dot(k, inner):
            dot_in(z, order(t * own_per_step + k))
            return inner

        lax.fori_loop(0, own_per_step, own_dot, 0)
        along(1, t)

        @pl.when(t > 0)
        def _():
            beside(1, t - 1)

        return carry

    lax.fori_loop(0, per, first, 0)

    def later(i, carry):
        dist = 2 + i // per
        t = lax.rem(i, per)
        along(dist, t)
        last = i + per - 1
        beside(1 + last // per, lax.rem(last, per))
        return carry

    if n_blk > 2:
        lax.fori_loop(0, per * (n_blk - 2), later, 0)
    beside(n_blk - 1, per - 1)

    for j in range(n_blk):
        part[j] = acc[j, 0, 0:count, :] + acc[j, 1, count:2 * count, :]

    def give(step):
        to, where = peer(step)
        return pltpu.make_async_remote_copy(
            src_ref=part.at[to],
            dst_ref=landed.at[step],
            send_sem=red_send.at[step],
            recv_sem=red_recv.at[step],
            device_id=where,
            device_id_type=MESH,
        )

    for step in range(1, n_red):
        give(step).start()

    examples = slab_hbm.shape[0]
    ids = qid_ref[pl.ds(rank, 1), :]
    q_hot = (
        jnp.broadcast_to(ids, (count, count))
        == lax.broadcasted_iota(jnp.int32, (count, count), 0)
    ).astype(F32)
    e_hot = (
        jnp.broadcast_to(eid_ref[...], (examples, examples))
        == lax.broadcasted_iota(jnp.int32, (examples, examples), 0)
    ).astype(F32)
    total = part[rank]
    for step in range(1, n_red):
        give(step).wait_recv()
        total = total + landed[step]
    total = total * (1.0 / PROJ**0.5)
    total = jnp.dot(q_hot, total, precision=lax.Precision.HIGHEST, preferred_element_type=F32)
    out_ref[...] = lax.dot_general(
        total, e_hot, (((1,), (1,)), ((), ())),
        precision=lax.Precision.HIGHEST, preferred_element_type=F32,
    )
    for step in range(1, n_red):
        give(step).wait_send()

    def drain(i, carry):
        j = i // per
        b = block_at(y, lax.rem(i, per))

        @pl.when((j >= z) & has_down)
        def _():
            move(j, b, 0).wait_send()

        @pl.when((j <= z) & has_up)
        def _():
            move(j, b, 1).wait_send()

        @pl.when(j != z)
        def _():
            for step in range(1, n_grp):
                move(j, b, 1 + step).wait_send()

        return carry

    lax.fori_loop(0, n_blk * per, drain, 0)


def local(sizes, queries, train_slab, basis_in, basis_out, eigvals, query_ids, example_ids):
    n_grp, n_blk, n_dim, n_sub = sizes
    count, width = queries.shape
    examples = train_slab.shape[0]
    blocks = basis_in.shape[0]
    n_red = n_dim * n_sub
    any_spec = pl.BlockSpec(memory_space=pl.ANY)
    vmem = pl.BlockSpec(memory_space=pltpu.VMEM)
    return pl.pallas_call(
        functools.partial(kernel, sizes),
        out_shape=jax.ShapeDtypeStruct((count, examples), F32),
        in_specs=[any_spec, any_spec, vmem, vmem, vmem, vmem, vmem],
        out_specs=vmem,
        scratch_shapes=[
            pltpu.VMEM((blocks, count, WIDE), BF16),
            pltpu.VMEM((examples, width), BF16),
            pltpu.VMEM((n_blk, blocks, 2 * count, HALF), BF16),
            pltpu.VMEM((n_blk, 2, 2 * count, examples), F32),
            pltpu.VMEM((count * TILES, 128), F32),
            pltpu.VMEM((SIDE, SIDE), F32),
            pltpu.VMEM((256, 256), BF16),
            pltpu.VMEM((n_blk, count, examples), F32),
            pltpu.VMEM((n_red, count, examples), F32),
            pltpu.SemaphoreType.DMA((blocks,)),
            pltpu.SemaphoreType.DMA((blocks,)),
            pltpu.SemaphoreType.DMA((n_blk, blocks)),
            pltpu.SemaphoreType.DMA((n_grp + 1, n_blk, blocks)),
            pltpu.SemaphoreType.DMA((n_red,)),
            pltpu.SemaphoreType.DMA((n_red,)),
        ],
        compiler_params=pltpu.CompilerParams(
            collective_id=0, has_side_effects=True, vmem_limit_bytes=50 * 1024 * 1024
        ),
    )(queries, train_slab, basis_in, basis_out, eigvals, query_ids, example_ids)


def solution(mesh):
    sizes = tuple(mesh.shape[name] for name in ("groups", "blk", "dim", "sub"))
    return jax.shard_map(
        functools.partial(local, sizes),
        mesh=mesh,
        in_specs=(
            P("blk", ("dim", "sub")),
            P(("groups", "blk"), ("dim", "sub")),
            P(("dim", "sub"), None, None),
            P(("dim", "sub"), None, None),
            P(("dim", "sub"), None, None),
            P(),
            P(("groups", "blk"), None),
        ),
        out_specs=P(("dim", "sub"), ("groups", "blk")),
        check_vma=False,
    )
```

time: 344 us -> 139 us (0.40)
  waiting for transfers between devices: 239 us -> 0 us
  Pallas kernels: 0 us -> 134 us
  matrix products: 59.3 us -> 0 us
  local copies, waits for them, and re-layouts: 30.7 us -> 4.88 us
  between operations: 13.5 us -> 0.01 us
    all_gather x1 -> x0, waiting for transfers between devices: 221 us -> none  [local(): lax.all_gather(ordered, 'blk', axis=0, tiled=True)]
    pallas_call x0 -> x1, Pallas kernels: none -> 134 us  [local(): pl.pallas_call(functools.partial(kernel, sizes), out_shape=jax.ShapeDtype...]
    dot_general x7 -> x0, matrix products: 59.3 us -> none  [the longest x1 12.8 us: precondition(): return jnp.einsum('qbae,bce->qbac', outer, right, precision=HIGH)]
    reshape x2 -> x0, local copies, waits for them, and re-layouts: 18.1 us -> none  [the longest x1 9.68 us: prepared(): precondition(blocks, basis_in, basis_out, eigvals).reshape(count, width)]
    unnamed x3 -> x0, waiting for transfers between devices: 17.8 us -> none
    transpose x1 -> x0, local copies, waits for them, and re-layouts: 11.8 us -> none  [precondition(): return jnp.einsum('qbae,bce->qbac', outer, right, precision=HIGH)]
    unnamed x8 -> x11, local copies, waits for them, and re-layouts: 0.02 us -> 4.88 us
  transfers between devices with their start and end apart: 2 -> 0, of which waited for: 2 -> 0; matrix products, arithmetic and copies ran while one was open for 0% -> 0% of each run, Pallas kernels for 0% -> 0%
where the time goes in v1:
time: 139 us; the launch traced here: 138 us
  Pallas kernels  134 us (96%)
  local copies, waits for them, and re-layouts  4.88 us (4%)
    pallas_call x1, Pallas kernels, local(): pl.pallas_call(functools.partial(kernel, sizes), out_shape=jax.ShapeDtype...  134 us
    unnamed x11, local copies, waits for them, and re-layouts  4.88 us

profile of v1, /device:TPU:0, one launch (start us, length us, event | category | flops | bytes accessed | tf_op | source)
XLA Modules:
  0.0 138.5 jit_solution(17560883684970460778)
XLA Ops:
  0.0 0.0 copy-start
  0.0 1.0 copy-done
  1.0 0.0 copy-start.1
  1.0 0.9 copy-done.1
  2.0 0.0 copy-start.2
  2.0 0.9 copy-done.2
  2.9 0.0 copy-start.3
  2.9 0.7 copy-done.3
  3.6 0.0 copy-start.4
  3.6 0.7 copy-done.4
  4.3 133.6 %shard_map.73 = f32[24,128]{1,0:T(8,128)S(1)} custom-call(bf16[24,65536]{1,0:T(8,128)(2,1)} %q_hbm.1, bf16[128,65536]{1,0:T(8,128)(2,1)} %slab_hbm.1, bf16[16,64,64]{2,1,0:T(8,128)(2,1)S(1)} %copy-done.1, bf16[16,64,64]{2,1,0:T(8,128)(2,1)S(1)} %copy-done.2, f32[16,64,64]{2,1,0:T(8,128)S(1)} %copy-done, s32[4,24]{1,0:T(4,128)S(1)} %copy-done.3, ...), custom_call_target="tpu_custom_call" | custom-call | tf_op jit(solution)/shard_map/pallas_call | solution.py:387
  137.9 0.6 copy.9
Async XLA Ops:
  0.0 1.0 copy-start
  1.0 0.9 copy-start.1
  2.0 0.9 copy-start.2
  2.9 0.7 copy-start.3
  3.6 0.7 copy-start.4

commit v2 on v1

--- a/solution.py
+++ b/solution.py
@@ -24,15 +24,17 @@
 
 
 def kernel(
-    sizes,
-    q_hbm, slab_hbm, a_ref, g_ref, eig_ref, qid_ref, eid_ref,
+    sizes, plan,
+    q_hbm, slab_hbm, a_hbm, g_hbm, eig_hbm, qid_hbm, eid_hbm,
     out_ref,
     q_v, slab, gath, acc, spread, left32, wide, part, landed,
-    q_sem, slab_sem, recv_sem, send_sem, red_send, red_recv,
+    a_ref, g_ref, eig_ref, qid_ref, eid_ref, ext, accx, partx, landx,
+    q_sem, slab_sem, recv_sem, send_sem, red_send, red_recv, in_sem, ext_sem, ret_sem,
 ):
     n_grp, n_blk, n_dim, n_sub = sizes
+    n_off, n_dir = plan
     count = q_hbm.shape[0]
-    blocks = a_ref.shape[0]
+    blocks = a_hbm.shape[0]
     per = blocks // n_grp
     n_red = n_dim * n_sub
     y = lax.axis_index("groups")
@@ -42,6 +44,30 @@
     rank = dx * n_sub + core
     has_up = z < n_blk - 1
     has_down = z > 0
+    at_end = (z == 0) | (z == n_blk - 1)
+
+    def off(t):
+        return t >= per - n_off
+
+    def straight(t):
+        return t >= per - n_dir
+
+    def inside(j):
+        return (z > 0) & (z < n_blk - 1) & (j > 0) & (j < n_blk - 1) & (
+            (j == z + 1) | (j == z - 1)
+        )
+
+    def goes_down(j, t):
+        return has_down & (j >= z) & jnp.logical_not((z == 1) & off(t))
+
+    def goes_up(j, t):
+        return has_up & (j <= z) & jnp.logical_not((z == n_blk - 2) & off(t))
+
+    def comes(j, t):
+        return (j >= 0) & (j < n_blk) & jnp.logical_not(at_end & off(t))
+
+    def crosses(j, t):
+        return comes(j, t) & jnp.logical_not(inside(j) & straight(t))
 
     def block_at(plane, t):
         return t * n_grp + plane
@@ -57,7 +83,10 @@
 
     def order(i):
         turn = i // per
-        return block_at(lax.rem(y + turn, n_grp), i - turn * per)
+        t = i - turn * per
+        if n_dir:
+            t = jnp.where(turn == 0, t, lax.rem(t + per - n_dir, per))
+        return block_at(lax.rem(y + turn, n_grp), t)
 
     def start_query(i, carry):
         query_copy(order(i)).start()
@@ -67,9 +96,6 @@
         slab_copy(order(i)).start()
         return carry
 
-    lax.fori_loop(0, blocks, start_query, 0)
-    lax.fori_loop(0, blocks, start_slab, 0)
-
     barrier = pltpu.get_barrier_semaphore()
 
     @pl.when(has_up)
@@ -92,8 +118,22 @@
     for step in range(1, n_red):
         pl.semaphore_signal(barrier, inc=1, device_id=peer(step)[1], device_id_type=MESH)
 
+    query_copy(order(0)).start()
+    small = [
+        pltpu.make_async_copy(src, dst, in_sem.at[k])
+        for k, (src, dst) in enumerate(
+            ((a_hbm, a_ref), (g_hbm, g_ref), (eig_hbm, eig_ref), (qid_hbm, qid_ref), (eid_hbm, eid_ref))
+        )
+    ]
+    for copy in small:
+        copy.start()
+    lax.fori_loop(1, blocks, start_query, 0)
+    lax.fori_loop(0, blocks, start_slab, 0)
     acc[...] = jnp.zeros_like(acc)
+    accx[...] = jnp.zeros_like(accx)
     wide[...] = jnp.zeros_like(wide)
+    for copy in small:
+        copy.wait()
 
     def precondition(b):
         query_copy(b).wait()
@@ -183,6 +223,14 @@
                 value, right, (((1,), (1,)), ((), ())), preferred_element_type=F32
             )
 
+    def dot_for_end(j, k, b):
+        value = gath[j, b]
+        for h in range(2):
+            accx[j, h] += lax.dot_general(
+                value, ext[k, :, h * HALF:(h + 1) * HALF], (((1,), (1,)), ((), ())),
+                preferred_element_type=F32,
+            )
+
     def move(j, b, way):
         if way == 0:
             to = {"blk": z - 1}
@@ -199,38 +247,42 @@
             device_id_type=MESH,
         )
 
-    def across(j, b):
-        for step in range(1, n_grp):
-            move(j, b, 1 + step).start()
-
-    def along(dist, t):
+    def across(j, t):
+        @pl.when(crosses(j, t))
+        def _():
+            for step in range(1, n_grp):
+                move(j, block_at(y, t), 1 + step).start()
+
+    def along(dist, t, ready):
         b = block_at(y, t)
 
-        @pl.when(z + dist < n_blk)
+        @pl.when(comes(z + dist, t))
         def _():
             move(z + dist, b, 0).wait_recv()
 
-            @pl.when(has_down)
+            @pl.when(goes_down(z + dist, t))
             def _():
                 move(z + dist, b, 0).start()
 
-            across(z + dist, b)
-
-        @pl.when(z - dist >= 0)
+            across(z + dist, t)
+
+        @pl.when(comes(z - dist, t))
         def _():
             move(z - dist, b, 1).wait_recv()
 
-            @pl.when(has_up)
+            @pl.when(goes_up(z - dist, t))
             def _():
                 move(z - dist, b, 1).start()
 
-            across(z - dist, b)
-
-        @pl.when(z + dist < n_blk)
+            across(z - dist, t)
+
+        ready()
+
+        @pl.when(comes(z + dist, t))
         def _():
             dot_in(z + dist, b)
 
-        @pl.when(z - dist >= 0)
+        @pl.when(comes(z - dist, t))
         def _():
             dot_in(z - dist, b)
 
@@ -238,61 +290,87 @@
         for step in range(1, n_grp):
             b = block_at(lax.rem(y + step, n_grp), t)
 
-            @pl.when(z + dist < n_blk)
+            @pl.when(crosses(z + dist, t))
             def _():
                 move(z + dist, b, 2).wait_recv()
                 dot_in(z + dist, b)
 
-            @pl.when(z - dist >= 0)
+            @pl.when(crosses(z - dist, t))
             def _():
                 move(z - dist, b, 2).wait_recv()
                 dot_in(z - dist, b)
 
-    def send_own(b):
-        @pl.when(has_down)
+    def send_own(i):
+        b = order(i)
+
+        @pl.when((i < per) & goes_down(z, i))
         def _():
             move(z, b, 0).start()
 
-        @pl.when(has_up)
+        @pl.when((i < per) & goes_up(z, i))
         def _():
             move(z, b, 1).start()
 
-    def own(i):
-        b = order(i)
-        precondition(b)
-
-        @pl.when(i < per)
-        def _():
-            send_own(b)
-
-        return b
-
+        if n_dir:
+            direct = (i >= per) & (i < per + n_dir)
+
+            @pl.when(direct & inside(z - 1))
+            def _():
+                move(z, b, 0).start()
+
+            @pl.when(direct & inside(z + 1))
+            def _():
+                move(z, b, 1).start()
+
+    def slab_move(k, plane, t):
+        b = block_at(plane, t)
+        return pltpu.make_async_remote_copy(
+            src_ref=slab_hbm.at[:, pl.ds(pl.multiple_of(b * WIDE, WIDE), WIDE)],
+            dst_ref=ext.at[k],
+            send_sem=ext_sem.at[0, k],
+            recv_sem=ext_sem.at[1, k],
+            device_id={"blk": jnp.where(z == 0, 1, n_blk - 2)},
+            device_id_type=MESH,
+        )
+
+    handed = [(g * n_off + k, g, per - n_off + k) for g in range(n_grp) for k in range(n_off)]
+
+    precondition(order(0))
     entry = n_grp - 1 + n_red - 1
     pl.semaphore_wait(barrier, entry + has_up.astype(jnp.int32) + has_down.astype(jnp.int32))
+    send_own(0)
 
     own_per_step = blocks // per
 
     def first(t, carry):
         def one(k, inner):
-            own(t * own_per_step + k)
+            i = t * own_per_step + k
+
+            @pl.when(i > 0)
+            def _():
+                precondition(order(i))
+                send_own(i)
+
             return inner
 
         lax.fori_loop(0, own_per_step, one, 0)
 
-        @pl.when(t == 0)
-        def _():
-            def wait_slab(i, inner):
-                slab_copy(order(i)).wait()
-                return inner
-
-            lax.fori_loop(0, blocks, wait_slab, 0)
-
-        def own_dot(k, inner):
-            dot_in(z, order(t * own_per_step + k))
-            return inner
-
-        lax.fori_loop(0, own_per_step, own_dot, 0)
-        along(1, t)
+        if n_off:
+            @pl.when((t == per // 2) & at_end)
+            def _():
+                for k, g, u in handed:
+                    slab_move(k, g, u).start()
+
+        def ready():
+            @pl.when(t == 0)
+            def _():
+                def wait_slab(i, inner):
+                    slab_copy(order(i)).wait()
+                    return inner
+
+                lax.fori_loop(0, blocks, wait_slab, 0)
+
+        along(1, t, ready)
 
         @pl.when(t > 0)
         def _():
@@ -301,21 +379,82 @@
         return carry
 
     lax.fori_loop(0, per, first, 0)
+
+    def nothing():
+        return None
+
+    def own_dot(i, carry):
+        dot_in(z, order(i))
+        return carry
 
     def later(i, carry):
         dist = 2 + i // per
         t = lax.rem(i, per)
-        along(dist, t)
+        along(dist, t, nothing)
         last = i + per - 1
         beside(1 + last // per, lax.rem(last, per))
+
+        @pl.when(i < blocks)
+        def _():
+            own_dot(i, 0)
+
         return carry
 
-    if n_blk > 2:
-        lax.fori_loop(0, per * (n_blk - 2), later, 0)
+    steps = per * (n_blk - 2)
+    if steps:
+        lax.fori_loop(0, steps, later, 0)
+    if steps < blocks:
+        lax.fori_loop(steps, blocks, own_dot, 0)
     beside(n_blk - 1, per - 1)
+
+    def to_end():
+        return pltpu.make_async_remote_copy(
+            src_ref=partx,
+            dst_ref=landx,
+            send_sem=ret_sem.at[0],
+            recv_sem=ret_sem.at[1],
+            device_id={"blk": jnp.where(z == 1, 0, n_blk - 1)},
+            device_id_type=MESH,
+        )
+
+    if n_dir:
+        def direct_in(j):
+            @pl.when(inside(j))
+            def _():
+                for t in range(per - n_dir, per):
+                    for step in range(1, n_grp):
+                        b = block_at(lax.rem(y + step, n_grp), t)
+                        move(j, b, 0).wait_recv()
+                        dot_in(j, b)
+
+        direct_in(z + 1)
+        direct_in(z - 1)
+
+    if n_off:
+        next_to_end = (z == 1) | (z == n_blk - 2)
+        end = jnp.where(z == 1, 0, n_blk - 1)
+
+        @pl.when(next_to_end)
+        def _():
+            for k, g, u in handed:
+                slab_move(k, g, u).wait_recv()
+                for j in range(n_blk):
+                    @pl.when(j != end)
+                    def _():
+                        dot_for_end(j, k, block_at(g, u))
+
+            for j in range(n_blk):
+                partx[j] = accx[j, 0, 0:count, :] + accx[j, 1, count:2 * count, :]
+            to_end().start()
 
     for j in range(n_blk):
         part[j] = acc[j, 0, 0:count, :] + acc[j, 1, count:2 * count, :]
+
+    if n_off:
+        @pl.when(at_end)
+        def _():
+            to_end().wait_recv()
+            part[...] += landx[...]
 
     def give(step):
         to, where = peer(step)
@@ -356,17 +495,18 @@
 
     def drain(i, carry):
         j = i // per
-        b = block_at(y, lax.rem(i, per))
-
-        @pl.when((j >= z) & has_down)
+        t = lax.rem(i, per)
+        b = block_at(y, t)
+
+        @pl.when(goes_down(j, t))
         def _():
             move(j, b, 0).wait_send()
 
-        @pl.when((j <= z) & has_up)
+        @pl.when(goes_up(j, t))
         def _():
             move(j, b, 1).wait_send()
 
-        @pl.when(j != z)
+        @pl.when((j != z) & crosses(j, t))
         def _():
             for step in range(1, n_grp):
                 move(j, b, 1 + step).wait_send()
@@ -374,6 +514,28 @@
         return carry
 
     lax.fori_loop(0, n_blk * per, drain, 0)
+
+    if n_dir:
+        for t in range(per - n_dir, per):
+            b = block_at(lax.rem(y + 1, n_grp), t)
+
+            @pl.when(inside(z - 1))
+            def _():
+                move(z, b, 0).wait_send()
+
+            @pl.when(inside(z + 1))
+            def _():
+                move(z, b, 1).wait_send()
+
+    if n_off:
+        @pl.when(at_end)
+        def _():
+            for k, g, u in handed:
+                slab_move(k, g, u).wait_send()
+
+        @pl.when(next_to_end)
+        def _():
+            to_end().wait_send()
 
 
 def local(sizes, queries, train_slab, basis_in, basis_out, eigvals, query_ids, example_ids):
@@ -382,12 +544,16 @@
     examples = train_slab.shape[0]
     blocks = basis_in.shape[0]
     n_red = n_dim * n_sub
+    per = blocks // n_grp
+    n_off = per // 8 if n_blk >= 4 and n_grp == 2 else 0
+    n_dir = per // 2 if n_off else 0
+    handed = max(1, n_off * n_grp)
     any_spec = pl.BlockSpec(memory_space=pl.ANY)
     vmem = pl.BlockSpec(memory_space=pltpu.VMEM)
     return pl.pallas_call(
-        functools.partial(kernel, sizes),
+        functools.partial(kernel, sizes, (n_off, n_dir)),
         out_shape=jax.ShapeDtypeStruct((count, examples), F32),
-        in_specs=[any_spec, any_spec, vmem, vmem, vmem, vmem, vmem],
+        in_specs=[any_spec] * 7,
         out_specs=vmem,
         scratch_shapes=[
             pltpu.VMEM((blocks, count, WIDE), BF16),
@@ -399,15 +565,27 @@
             pltpu.VMEM((256, 256), BF16),
             pltpu.VMEM((n_blk, count, examples), F32),
             pltpu.VMEM((n_red, count, examples), F32),
+            pltpu.VMEM(basis_in.shape, BF16),
+            pltpu.VMEM(basis_out.shape, BF16),
+            pltpu.VMEM(eigvals.shape, F32),
+            pltpu.VMEM(query_ids.shape, jnp.int32),
+            pltpu.VMEM(example_ids.shape, jnp.int32),
+            pltpu.VMEM((handed, examples, WIDE), BF16),
+            pltpu.VMEM((n_blk, 2, 2 * count, examples), F32),
+            pltpu.VMEM((n_blk, count, examples), F32),
+            pltpu.VMEM((n_blk, count, examples), F32),
             pltpu.SemaphoreType.DMA((blocks,)),
             pltpu.SemaphoreType.DMA((blocks,)),
             pltpu.SemaphoreType.DMA((n_blk, blocks)),
             pltpu.SemaphoreType.DMA((n_grp + 1, n_blk, blocks)),
             pltpu.SemaphoreType.DMA((n_red,)),
             pltpu.SemaphoreType.DMA((n_red,)),
+            pltpu.SemaphoreType.DMA((5,)),
+            pltpu.SemaphoreType.DMA((2, handed)),
+            pltpu.SemaphoreType.DMA((2,)),
         ],
         compiler_params=pltpu.CompilerParams(
-            collective_id=0, has_side_effects=True, vmem_limit_bytes=50 * 1024 * 1024
+            collective_id=0, has_side_effects=True, vmem_limit_bytes=64 * 1024 * 1024 - 65536
         ),
     )(queries, train_slab, basis_in, basis_out, eigvals, query_ids, example_ids)
 

time: 139 us -> 124 us (0.89)
  Pallas kernels: 134 us -> 123 us
  local copies, waits for them, and re-layouts: 4.88 us -> 1.31 us
    pallas_call x1, Pallas kernels: 134 us -> 123 us  [local(): pl.pallas_call(functools.partial(kernel, sizes, (n_off, n_dir)), out_shap...]
    unnamed x11 -> x1, local copies, waits for them, and re-layouts: 4.88 us -> 1.31 us
where the time goes in v2:
time: 124 us
  Pallas kernels  123 us (99%)
  local copies, waits for them, and re-layouts  1.31 us (1%)
    pallas_call x1, Pallas kernels, local(): pl.pallas_call(functools.partial(kernel, sizes, (n_off, n_dir)), out_shap...  123 us

profile of v2, /device:TPU:0, one launch (start us, length us, event | category | flops | bytes accessed | tf_op | source)
XLA Modules:
  0.0 123.8 jit_solution(3765388306293048945)
XLA Ops:
  0.0 122.5 %shard_map.73 = f32[24,128]{1,0:T(8,128)} custom-call(bf16[24,65536]{1,0:T(8,128)(2,1)} %q_hbm.1, bf16[128,65536]{1,0:T(8,128)(2,1)} %slab_hbm.1, bf16[16,64,64]{2,1,0:T(8,128)(2,1)} %a_hbm.1, bf16[16,64,64]{2,1,0:T(8,128)(2,1)} %g_hbm.1, f32[16,64,64]{2,1,0:T(8,128)} %eig_hbm.1, s32[4,24]{1,0:T(4,128)} %qid_hbm.1, s32[1,128]{1,0:T(1,128)} %eid_hbm.1), custom_call_target="tpu_custom_call" | custom-call | tf_op jit(solution)/shard_map/pallas_call | solution.py:553
  122.5 1.3 %copy.9 = f32[24,128]{1,0:T(8,128)} copy(f32[24,128]{1,0:T(8,128)} %shard_map.73) | data formatting | bytes 24576

commit v3 on v2

--- a/solution.py
+++ b/solution.py
@@ -311,17 +311,6 @@
         def _():
             move(z, b, 1).start()
 
-        if n_dir:
-            direct = (i >= per) & (i < per + n_dir)
-
-            @pl.when(direct & inside(z - 1))
-            def _():
-                move(z, b, 0).start()
-
-            @pl.when(direct & inside(z + 1))
-            def _():
-                move(z, b, 1).start()
-
     def slab_move(k, plane, t):
         b = block_at(plane, t)
         return pltpu.make_async_remote_copy(
@@ -399,6 +388,18 @@
             own_dot(i, 0)
 
         return carry
+
+    if n_dir:
+        for t in range(per - n_dir, per):
+            b = block_at(lax.rem(y + 1, n_grp), t)
+
+            @pl.when(inside(z - 1))
+            def _():
+                move(z, b, 0).start()
+
+            @pl.when(inside(z + 1))
+            def _():
+                move(z, b, 1).start()
 
     steps = per * (n_blk - 2)
     if steps:

time: 124 us -> 124 us (level)
  no operation moved by 1% of the time
where the time goes in v3:
time: 124 us
  Pallas kernels  123 us (99%)
  local copies, waits for them, and re-layouts  1.31 us (1%)
    pallas_call x1, Pallas kernels, local(): pl.pallas_call(functools.partial(kernel, sizes, (n_off, n_dir)), out_shap...  123 us

profile of v3, /device:TPU:0, one launch (start us, length us, event | category | flops | bytes accessed | tf_op | source)
XLA Modules:
  0.0 123.9 jit_solution(16795464452415187837)
XLA Ops:
  0.0 122.6 %shard_map.73 = f32[24,128]{1,0:T(8,128)} custom-call(bf16[24,65536]{1,0:T(8,128)(2,1)} %q_hbm.1, bf16[128,65536]{1,0:T(8,128)(2,1)} %slab_hbm.1, bf16[16,64,64]{2,1,0:T(8,128)(2,1)} %a_hbm.1, bf16[16,64,64]{2,1,0:T(8,128)(2,1)} %g_hbm.1, f32[16,64,64]{2,1,0:T(8,128)} %eig_hbm.1, s32[4,24]{1,0:T(4,128)} %qid_hbm.1, s32[1,128]{1,0:T(1,128)} %eid_hbm.1), custom_call_target="tpu_custom_call" | custom-call | tf_op jit(solution)/shard_map/pallas_call | solution.py:554
  122.6 1.3 %copy.9 = f32[24,128]{1,0:T(8,128)} copy(f32[24,128]{1,0:T(8,128)} %shard_map.73) | data formatting | bytes 24576
